TPU v7x, 512 devices: a whole 4x4x16 slice. The times are simulated.
512 devices in a mesh: half: 2 (over core), row: 16 (over z), col: 16 (over y, x).
Axes of the slice: x: 4, y: 4, z: 16, core: 2. Of those that a mesh axis runs over, the one named last changes fastest.
Arguments:
- child_front: float32 [2, 8192, 8192], P('half', 'row', 'col'), as said below
- child_map: int32 [2, 48], P('half'), may hold values from 0 to 63, as said below
- root_front: float32 [8192, 16, 2, 256], P('row', 'col', 'half'), as said below
Outputs:
- child_panel: float32 [2, 512, 8192], P('half', None, 'col')
- root_panel: float32 [512, 16, 2, 256], P(None, 'col', 'half')
- root_update: float32 [8192, 16, 2, 256], P('row', 'col', 'half')
Inputs may be any that keep to these rules, and one draw needn't show every extreme that they name: `child_map`: for child h, the update blocks of row part k (the 3 blocks after that part's first block) map in increasing order to distinct blocks among the root's blocks k * 4 to (k + 1) * 4 - 1. `child_front`: each child's front is symmetric and positive definite. `root_front`: the root front is symmetric and positive definite.
All inputs are finite; a program needn't handle non-finite values.
Results may differ from a plain program's by a relative error of at most 0.0001.
Values sent between devices are 32-bit elements; how exact they have to be, the bound alone decides.
A program may use at most 64 MiB of HBM per device.

v0:
```python
import jax
import jax.numpy as jnp
from jax import lax
from jax.sharding import PartitionSpec as P

BLK = 128
PB = 32


def spread_2(value, axis, source):
    kept = jnp.where(lax.axis_index(axis) == source, value, 0).astype(value.dtype)
    return lax.psum(kept, axis)


def lower_solve(factor, right):
    return lax.linalg.triangular_solve(factor, right, left_side=True, lower=True)


def transposed_product(left, right):
    return lax.dot_general(
        left,
        right,
        (((0,), (0,)), ((), ())),
        precision=lax.Precision.HIGHEST,
        preferred_element_type=jnp.float32,
    )


def selector(child_row_map, part_index, child_tiles, root_tiles):
    per_part = child_tiles - 1
    targets = (
        lax.dynamic_slice_in_dim(child_row_map, part_index * per_part, per_part)
        - part_index * root_tiles
    )
    one_hot = (jnp.arange(root_tiles, dtype=jnp.int32)[:, None] == targets[None, :]).astype(
        jnp.float32
    )
    return jnp.concatenate([jnp.zeros((root_tiles, 1), jnp.float32), one_hot], axis=1)


def body(child_front, child_map, root_front):
    tile_rows = BLK
    pivot_count = PB
    child_block = child_front[0]
    part_rows = child_block.shape[0]
    row_part = lax.axis_index("row")
    col_part = lax.axis_index("col")
    strips = lax.all_gather(child_block[:pivot_count, :], "row", axis=0, tiled=True)
    pieces = lax.all_gather(
        child_block[None, :pivot_count, :pivot_count], ("row", "col"), axis=0, tiled=True
    )
    parts_count = lax.axis_size("row")
    corner = pieces.reshape(parts_count, parts_count, pivot_count, pivot_count).transpose(
        0, 2, 1, 3
    )
    corner = corner.reshape(parts_count * pivot_count, parts_count * pivot_count)
    factor = jnp.linalg.cholesky(corner)
    child_panel = lower_solve(factor, strips)
    columns = lax.all_gather(child_block[:, :pivot_count], "col", axis=1, tiled=True)
    panel_rows = lower_solve(factor, columns.T)
    update = child_block - transposed_product(panel_rows, child_panel)
    root_rows = root_front.shape[0]
    child_tiles = part_rows // tile_rows
    root_tiles = root_rows // tile_rows
    own_map = child_map[0]
    row_select = selector(own_map, row_part, child_tiles, root_tiles)
    col_select = selector(own_map, col_part, child_tiles, root_tiles)
    blocks = update.reshape(child_tiles, tile_rows, child_tiles, tile_rows)
    spread = jnp.einsum("ap,piqj->aiqj", row_select, blocks, precision=lax.Precision.HIGHEST)
    spread = jnp.einsum("aiqj,bq->aibj", spread, col_select, precision=lax.Precision.HIGHEST)
    additions = spread.reshape(root_rows, 2, root_rows // 2)
    joined = lax.psum_scatter(additions, "half", scatter_dimension=1, tiled=True)
    assembled = root_front[:, 0, 0, :] + joined[:, 0, :]
    root_strips = lax.all_gather(assembled[:pivot_count, :], "row", axis=0, tiled=True)
    pivots = spread_2(root_strips[:, :pivot_count], "half", 0)
    root_corner = lax.all_gather(pivots, "col", axis=1, tiled=True)
    root_factor = jnp.linalg.cholesky(root_corner)
    root_panel = lower_solve(root_factor, root_strips)
    mirrored = spread_2(root_panel, "col", row_part)
    both_halves = lax.all_gather(mirrored[:, None, :], "half", axis=1, tiled=True)
    panel_side = both_halves.reshape(both_halves.shape[0], root_rows)
    root_update = assembled - transposed_product(panel_side, root_panel)
    return (child_panel[None], root_panel[:, None, None, :], root_update[:, None, None, :])


def solution(mesh):
    return jax.shard_map(
        body,
        mesh=mesh,
        in_specs=(P("half", "row", "col"), P("half", None), P("row", "col", "half", None)),
        out_specs=(
            P("half", None, "col"),
            P(None, "col", "half", None),
            P("row", "col", "half", None),
        ),
        check_vma=False,
    )
```

profile of v0, /device:TPU:1, one launch (start us, length us, event | category | flops | bytes accessed | tf_op | source)
XLA Modules:
  0.0 844.2 jit_solution(4435899986150828886)
XLA Ops:
  12.8 208.7 %all-gather.14.cloned.1.call-done = f32[8192,32]{1,0:T(8,128)} async-done(((f32[32,32]{1,0:T(8,128)}), f32[8192,32]{1,0:T(8,128)}) %all-gather.14.cloned.1.call-update) | async-done | bytes 1048592 | tf_op jit(solution)/shard_map/all_gather | solution.py:49
  221.5 5.6 copy.23
  227.1 3.5 reshape.68
  232.2 11.7 %cholesky.286 = f32[128,128]{1,0:T(8,128)S(1)} custom-call(f32[128,128]{1,0:T(8,128)S(1)} %cholesky.426), custom_call_target="Cholesky" | custom-call | tf_op jit(solution)/shard_map/jit(cholesky)/cholesky | solution.py:57
  244.0 9.8 %custom-call.31 = f32[1,128,128]{1,2,0:T(8,128)S(1)} custom-call(f32[1,128,128]{2,1,0:T(8,128)S(1)} %get-tuple-element.79), custom_call_target="InvertDiagBlocksLowerTriangular" | custom-call | tf_op jit(solution)/shard_map/jit(cholesky)/cholesky | solution.py:57
  256.4 11.7 %cholesky.305 = f32[128,128]{1,0:T(8,128)S(1)} custom-call(f32[128,128]{1,0:T(8,128)S(1)} %cholesky.430), custom_call_target="Cholesky" | custom-call | tf_op jit(solution)/shard_map/jit(cholesky)/cholesky | solution.py:57
  268.2 10.0 %custom-call.32 = f32[1,128,128]{1,2,0:T(8,128)S(1)} custom-call(f32[1,128,128]{2,1,0:T(8,128)S(1)} %get-tuple-element.76), custom_call_target="InvertDiagBlocksLowerTriangular" | custom-call | tf_op jit(solution)/shard_map/jit(cholesky)/cholesky | solution.py:57
  279.7 11.7 %cholesky.326 = f32[128,128]{1,0:T(8,128)S(1)} custom-call(f32[128,128]{1,0:T(8,128)S(1)} %cholesky.435), custom_call_target="Cholesky" | custom-call | tf_op jit(solution)/shard_map/jit(cholesky)/cholesky | solution.py:57
  292.2 9.8 %custom-call.33 = f32[1,128,128]{1,2,0:T(8,128)S(1)} custom-call(f32[1,128,128]{2,1,0:T(8,128)S(1)} %get-tuple-element.73), custom_call_target="InvertDiagBlocksLowerTriangular" | custom-call | tf_op jit(solution)/shard_map/jit(cholesky)/cholesky | solution.py:57
  303.5 11.7 %cholesky.343 = f32[128,128]{1,0:T(8,128)S(1)} custom-call(f32[128,128]{1,0:T(8,128)S(1)} %convolution_subtract_fusion.16), custom_call_target="Cholesky" | custom-call | tf_op jit(solution)/shard_map/jit(cholesky)/cholesky | solution.py:57
  319.6 8.5 %while.6 = (s32[]{:T(128)}, f32[512,512]{1,0:T(8,128)S(1)}, s32[4,2]{0,1:T(2,128)S(1)}, f32[4,128,128]{2,1,0:T(8,128)S(1)}, s32[]{:T(128)}) while((s32[]{:T(128)}, f32[512,512]{1,0:T(8,128)S(1)}, s32[4,2]{0,1:T(2,128)S(1)}, f32[4,128,128]{2,1,0:T(8,128)S(1)}, s32[]{:T(128)}) %tuple.64), condition=%wide.while_cond, body=%wide.while_body.sunk | while | flops 2 | bytes 131181 | solution.py:16
  328.1 39.3 %custom-call.34 = f32[4,128,128]{1,2,0:T(8,128)S(1)} custom-call(f32[4,128,128]{2,1,0:T(8,128)S(1)} %get-tuple-element.27), custom_call_target="InvertDiagBlocksLowerTriangular" | custom-call | tf_op jit(solution)/shard_map/triangular_solve/custom-call.3 | solution.py:16
  373.1 1.6 convolution_subtract_fusion.6
  380.8 1.6 convolution_subtract_fusion.7
  383.6 3.1 convolution_subtract_fusion
  387.0 1.7 fusion.11
  392.0 23.3 %reduce-scatter.2.cloned.1.call-done = f32[512,1,256]{2,0,1:T(8,128)} async-done(((f32[512,2,256]{2,0,1:T(8,128)}), f32[512,1,256]{2,0,1:T(8,128)}) %reduce-scatter.2.cloned.1.call-update) | async-done | bytes 524304 | tf_op jit(solution)/shard_map/reduce_scatter | solution.py:72
  417.2 25.4 %all_gather.21 = f32[512,256]{1,0:T(8,128)S(1)} all-gather(f32[32,256]{1,0:T(8,128)S(1)} %slice.211), channel_id=1, replica_groups=mesh['half'=2,'row'=16,'col'=16] {'row'}, dimensions={0}, use_global_device_ids=true | all-gather | bytes 557056 | tf_op jit(solution)/shard_map/all_gather | solution.py:74
  443.4 44.3 %all-reduce.6.cloned.1.call-done = f32[512,32]{0,1:T(8,128)} async-done(((f32[512,32]{0,1:T(8,128)}), f32[512,32]{0,1:T(8,128)}) %all-reduce.6.cloned.1.call-update) | async-done | bytes 65552 | tf_op jit(solution)/shard_map/psum | solution.py:12
  487.9 59.6 %all-gather.10.cloned.1.call-done = f32[512,512]{0,1:T(8,128)} async-done(((f32[512,32]{0,1:T(8,128)}), f32[512,512]{0,1:T(8,128)}) %all-gather.10.cloned.1.call-update) | async-done | bytes 1048592 | tf_op jit(solution)/shard_map/all_gather | solution.py:76
  550.5 11.7 %cholesky.358 = f32[128,128]{1,0:T(8,128)S(1)} custom-call(f32[128,128]{1,0:T(8,128)S(1)} %cholesky.439), custom_call_target="Cholesky" | custom-call | tf_op jit(solution)/shard_map/jit(cholesky)/cholesky | solution.py:77
  562.4 9.8 %custom-call.36 = f32[1,128,128]{1,2,0:T(8,128)S(1)} custom-call(f32[1,128,128]{2,1,0:T(8,128)S(1)} %get-tuple-element.69), custom_call_target="InvertDiagBlocksLowerTriangular" | custom-call | tf_op jit(solution)/shard_map/jit(cholesky)/cholesky | solution.py:77
  573.6 11.7 %cholesky.377 = f32[128,128]{1,0:T(8,128)S(1)} custom-call(f32[128,128]{1,0:T(8,128)S(1)} %cholesky.443), custom_call_target="Cholesky" | custom-call | tf_op jit(solution)/shard_map/jit(cholesky)/cholesky | solution.py:77
  586.7 10.0 %custom-call.37 = f32[1,128,128]{1,2,0:T(8,128)S(1)} custom-call(f32[1,128,128]{2,1,0:T(8,128)S(1)} %get-tuple-element.66), custom_call_target="InvertDiagBlocksLowerTriangular" | custom-call | tf_op jit(solution)/shard_map/jit(cholesky)/cholesky | solution.py:77
  598.8 13.2 %cholesky.398 = f32[128,128]{1,0:T(8,128)} custom-call(f32[128,128]{1,0:T(8,128)} %cholesky.448), custom_call_target="Cholesky" | custom-call | tf_op jit(solution)/shard_map/jit(cholesky)/cholesky | solution.py:77
  614.2 11.3 %custom-call.38 = f32[1,128,128]{1,2,0:T(8,128)} custom-call(f32[1,128,128]{2,1,0:T(8,128)} %get-tuple-element.63), custom_call_target="InvertDiagBlocksLowerTriangular" | custom-call | tf_op jit(solution)/shard_map/jit(cholesky)/cholesky | solution.py:77
  626.9 11.7 %cholesky.415 = f32[128,128]{1,0:T(8,128)S(1)} custom-call(f32[128,128]{1,0:T(8,128)S(1)} %convolution_subtract_fusion.15), custom_call_target="Cholesky" | custom-call | tf_op jit(solution)/shard_map/jit(cholesky)/cholesky | solution.py:77
  642.2 8.0 while.5
  650.2 39.3 %custom-call.26 = f32[4,128,128]{1,2,0:T(8,128)S(1)} custom-call(f32[4,128,128]{2,1,0:T(8,128)S(1)} %get-tuple-element.20), custom_call_target="InvertDiagBlocksLowerTriangular" | custom-call | tf_op jit(solution)/shard_map/triangular_solve | solution.py:16
  693.7 115.5 %all-reduce.8.cloned.1.call-done = f32[512,1,256]{2,0,1:T(8,128)} async-done(((f32[512,1,256]{2,0,1:T(8,128)}), f32[512,1,256]{2,0,1:T(8,128)}) %all-reduce.8.cloned.1.call-update) | async-done | bytes 524304 | tf_op jit(solution)/shard_map/psum | solution.py:12
  809.2 2.0 fusion.23
  812.5 20.5 %all-gather.12.cloned.1.call-done = f32[512,2,256]{2,0,1:T(8,128)} async-done(((f32[512,1,256]{2,0,1:T(8,128)}), f32[512,2,256]{2,0,1:T(8,128)}) %all-gather.12.cloned.1.call-update) | async-done | bytes 1048592 | tf_op jit(solution)/shard_map/all_gather | solution.py:80
  (146 shorter events, 73.0 us)
Async XLA Ops:
  7.2 214.4 %all-gather.14.cloned.1.call-start = ((), (), s32[]{:S(2)}) async-start(), calls=%async_computation.7 | async-start | bytes 4210688 | tf_op jit(solution)/shard_map/all_gather | solution.py:49
  8.6 358.9 %all-gather.8.cloned.1.call-start = ((), (), s32[]{:S(2)}) async-start(), calls=%async_computation.1 | async-start | bytes 1114112 | tf_op jit(solution)/shard_map/all_gather | solution.py:59
  10.3 365.5 %all-gather.16.cloned.1.call-start = ((), (), s32[]{:S(2)}) async-start(), calls=%async_computation.8 | async-start | bytes 1114112 | tf_op jit(solution)/shard_map/all_gather | solution.py:48
  11.9 403.3 %reduce-scatter.2.cloned.1.call-start = ((), (), s32[]{:S(2)}) async-start(), calls=%async_computation.2 | async-start | bytes 1572864 | tf_op jit(solution)/shard_map/reduce_scatter | solution.py:72
  231.2 1.0 copy-start
  372.4 0.7 copy-start.3
  375.8 7.7 copy-start.4
  375.8 7.7 copy-start.9
  382.9 0.7 copy-start.5
  388.7 26.5 %copy-start.7 = (f32[512,1,1,256]{3,2,1,0:T(1,128)S(1)}, f32[512,1,1,256]{3,2,1,0:T(1,128)}, u32[]{:S(2)}) copy-start(f32[512,1,1,256]{3,2,1,0:T(1,128)} %param.8) | copy-start | bytes 1572868
  391.9 95.8 %all-reduce.6.cloned.1.call-start = ((), (), s32[]{:S(2)}) async-start(), calls=%async_computation.3 | async-start | bytes 131072 | tf_op jit(solution)/shard_map/psum | solution.py:12
  416.4 0.8 copy-start.1
  443.3 104.2 %all-gather.10.cloned.1.call-start = ((), (), s32[]{:S(2)}) async-start(), calls=%async_computation.4 | async-start | bytes 1114112 | tf_op jit(solution)/shard_map/all_gather | solution.py:76
  487.7 321.4 %all-reduce.8.cloned.1.call-start = ((), (), s32[]{:S(2)}) async-start(), calls=%async_computation.5 | async-start | bytes 1048576 | tf_op jit(solution)/shard_map/psum | solution.py:12
  572.9 0.7 copy-start.6
  689.6 1.5 copy-start.8
  691.5 143.1 %copy-start.2 = (f32[512,256]{1,0:T(8,128)S(1)}, f32[512,256]{1,0:T(8,128)}, u32[]{:S(2)}) copy-start(f32[512,256]{1,0:T(8,128)} %copy-done.1) | copy-start | bytes 1572868
  693.6 139.4 %all-gather.12.cloned.1.call-start = ((), (), s32[]{:S(2)}) async-start(), calls=%async_computation.6 | async-start | bytes 1572864 | tf_op jit(solution)/shard_map/all_gather | solution.py:80
Sparse Core Ops, SparseCore 0:
  13.1 208.4 all-gather.13
  225.1 59.4 all-gather.7
  287.2 63.2 all-gather.15
  392.0 23.1 reduce-scatter.1
  443.5 44.1 all-reduce.5
  491.0 56.4 all-gather.9
  693.7 115.3 all-reduce.7
  811.2 21.7 all-gather.11
where the time goes:
time: 855 us; the launch traced here: 844 us
  waiting for transfers between devices  472 us (55%)
  other arithmetic  248 us (29%)
  local copies, waits for them, and re-layouts  43.7 us (5%)
  matrix products  33.6 us (4%)
  blocking collectives  25.4 us (3%)
  between operations  20.3 us (2%)
    all_gather x1, waiting for transfers between devices, body(): lax.all_gather(child_block[None, :pivot_count, :pivot_count], ('row', 'co...  209 us
    psum x2, waiting for transfers between devices, spread_2(): return lax.psum(kept, axis)  160 us
    another operation x15, other arithmetic, body(): root_factor = jnp.linalg.cholesky(root_corner)  83.6 us
    another operation x5, other arithmetic, lower_solve(): lax.linalg.triangular_solve(factor, right, left_side=True, lower=True)  79.1 us
    another operation x14, other arithmetic, body(): factor = jnp.linalg.cholesky(corner)  78.6 us
    all_gather x1, waiting for transfers between devices, body(): root_corner = lax.all_gather(pivots, 'col', axis=1, tiled=True)  59.6 us
    all_gather x1, blocking collectives, body(): lax.all_gather(assembled[:pivot_count, :], 'row', axis=0, tiled=True)  25.4 us
    reduce_scatter x1, waiting for transfers between devices, body(): lax.psum_scatter(additions, 'half', scatter_dimension=1, tiled=True)  23.3 us
  transfers between devices with their start and end apart: 8, of which 6 were waited for; matrix products, arithmetic and copies ran while one was open for 19% of the time, Pallas kernels for 0%

commit v1 on v0

--- a/solution.py
+++ b/solution.py
@@ -5,6 +5,14 @@
 
 BLK = 128
 PB = 32
+
+
+def gather_from_all(shard, axis, dim):
+    size = lax.axis_size(axis)
+    repeats = [size if d == dim else 1 for d in range(shard.ndim)]
+    return lax.all_to_all(
+        jnp.tile(shard, repeats), axis, split_axis=dim, concat_axis=dim, tiled=True
+    )
 
 
 def spread_2(value, axis, source):
@@ -73,7 +81,7 @@
     assembled = root_front[:, 0, 0, :] + joined[:, 0, :]
     root_strips = lax.all_gather(assembled[:pivot_count, :], "row", axis=0, tiled=True)
     pivots = spread_2(root_strips[:, :pivot_count], "half", 0)
-    root_corner = lax.all_gather(pivots, "col", axis=1, tiled=True)
+    root_corner = gather_from_all(pivots, "col", 1)
     root_factor = jnp.linalg.cholesky(root_corner)
     root_panel = lower_solve(root_factor, root_strips)
     mirrored = spread_2(root_panel, "col", row_part)

time: 855 us -> 813 us (0.951)
  waiting for transfers between devices: 472 us -> 428 us
    all_gather x1 -> x0, waiting for transfers between devices: 59.6 us -> none  [body(): root_corner = lax.all_gather(pivots, 'col', axis=1, tiled=True)]
    all_to_all x0 -> x1, waiting for transfers between devices: none -> 16.3 us  [gather_from_all(): lax.all_to_all(jnp.tile(shard, repeats), axis, split_axis=dim, concat_axi...]
  transfers between devices with their start and end apart: 8 -> 8, of which waited for: 6 -> 6; matrix products, arithmetic and copies ran while one was open for 19% -> 20% of each run, Pallas kernels for 0% -> 0%
where the time goes in v1:
time: 813 us; the launch traced here: 802 us
  waiting for transfers between devices  428 us (53%)
  other arithmetic  243 us (30%)
  local copies, waits for them, and re-layouts  43.8 us (5%)
  matrix products  35.5 us (4%)
  blocking collectives  25.4 us (3%)
  between operations  20.3 us (2%)
    all_gather x1, waiting for transfers between devices, body(): lax.all_gather(child_block[None, :pivot_count, :pivot_count], ('row', 'co...  209 us
    psum x2, waiting for transfers between devices, spread_2(): return lax.psum(kept, axis)  159 us
    another operation x5, other arithmetic, lower_solve(): lax.linalg.triangular_solve(factor, right, left_side=True, lower=True)  79.5 us
    another operation x15, other arithmetic, body(): root_factor = jnp.linalg.cholesky(root_corner)  79.2 us
    another operation x14, other arithmetic, body(): factor = jnp.linalg.cholesky(corner)  78.6 us
    all_gather x1, blocking collectives, body(): lax.all_gather(assembled[:pivot_count, :], 'row', axis=0, tiled=True)  25.4 us
    reduce_scatter x1, waiting for transfers between devices, body(): lax.psum_scatter(additions, 'half', scatter_dimension=1, tiled=True)  23.3 us
    all_gather x1, waiting for transfers between devices, body(): lax.all_gather(mirrored[:, None, :], 'half', axis=1, tiled=True)  20.7 us
  transfers between devices with their start and end apart: 8, of which 6 were waited for; matrix products, arithmetic and copies ran while one was open for 20% of the time, Pallas kernels for 0%

profile of v1, /device:TPU:1, one launch (start us, length us, event | category | flops | bytes accessed | tf_op | source)
XLA Modules:
  0.0 802.4 jit_solution(15668333136225276405)
XLA Ops:
  12.8 208.7 %all-gather.11.cloned.1.call-done = f32[8192,32]{1,0:T(8,128)} async-done(((f32[32,32]{1,0:T(8,128)}), f32[8192,32]{1,0:T(8,128)}) %all-gather.11.cloned.1.call-update) | async-done | bytes 1048592 | tf_op jit(solution)/shard_map/all_gather | solution.py:57
  221.5 5.6 copy.21
  227.1 3.5 reshape.75
  232.2 11.7 %cholesky.286 = f32[128,128]{1,0:T(8,128)S(1)} custom-call(f32[128,128]{1,0:T(8,128)S(1)} %cholesky.426), custom_call_target="Cholesky" | custom-call | tf_op jit(solution)/shard_map/jit(cholesky)/cholesky | solution.py:65
  244.0 9.8 %custom-call.31 = f32[1,128,128]{1,2,0:T(8,128)S(1)} custom-call(f32[1,128,128]{2,1,0:T(8,128)S(1)} %get-tuple-element.79), custom_call_target="InvertDiagBlocksLowerTriangular" | custom-call | tf_op jit(solution)/shard_map/jit(cholesky)/cholesky | solution.py:65
  256.4 11.7 %cholesky.305 = f32[128,128]{1,0:T(8,128)S(1)} custom-call(f32[128,128]{1,0:T(8,128)S(1)} %cholesky.430), custom_call_target="Cholesky" | custom-call | tf_op jit(solution)/shard_map/jit(cholesky)/cholesky | solution.py:65
  268.2 10.0 %custom-call.32 = f32[1,128,128]{1,2,0:T(8,128)S(1)} custom-call(f32[1,128,128]{2,1,0:T(8,128)S(1)} %get-tuple-element.76), custom_call_target="InvertDiagBlocksLowerTriangular" | custom-call | tf_op jit(solution)/shard_map/jit(cholesky)/cholesky | solution.py:65
  279.7 11.7 %cholesky.326 = f32[128,128]{1,0:T(8,128)S(1)} custom-call(f32[128,128]{1,0:T(8,128)S(1)} %cholesky.435), custom_call_target="Cholesky" | custom-call | tf_op jit(solution)/shard_map/jit(cholesky)/cholesky | solution.py:65
  292.2 9.8 %custom-call.33 = f32[1,128,128]{1,2,0:T(8,128)S(1)} custom-call(f32[1,128,128]{2,1,0:T(8,128)S(1)} %get-tuple-element.73), custom_call_target="InvertDiagBlocksLowerTriangular" | custom-call | tf_op jit(solution)/shard_map/jit(cholesky)/cholesky | solution.py:65
  303.5 11.7 %cholesky.343 = f32[128,128]{1,0:T(8,128)S(1)} custom-call(f32[128,128]{1,0:T(8,128)S(1)} %convolution_subtract_fusion.16), custom_call_target="Cholesky" | custom-call | tf_op jit(solution)/shard_map/jit(cholesky)/cholesky | solution.py:65
  319.2 8.5 %while.6 = (s32[]{:T(128)}, f32[512,512]{1,0:T(8,128)S(1)}, s32[4,2]{0,1:T(2,128)S(1)}, f32[4,128,128]{2,1,0:T(8,128)S(1)}, s32[]{:T(128)}) while((s32[]{:T(128)}, f32[512,512]{1,0:T(8,128)S(1)}, s32[4,2]{0,1:T(2,128)S(1)}, f32[4,128,128]{2,1,0:T(8,128)S(1)}, s32[]{:T(128)}) %tuple.64), condition=%wide.while_cond, body=%wide.while_body.sunk | while | flops 2 | bytes 131181 | solution.py:24
  327.7 39.7 %custom-call.34 = f32[4,128,128]{1,2,0:T(8,128)S(1)} custom-call(f32[4,128,128]{2,1,0:T(8,128)S(1)} %get-tuple-element.27), custom_call_target="InvertDiagBlocksLowerTriangular" | custom-call | tf_op jit(solution)/shard_map/triangular_solve/custom-call.3 | solution.py:24
  380.8 1.6 convolution_subtract_fusion.7
  383.6 3.1 convolution_subtract_fusion
  387.0 1.7 fusion.11
  392.0 23.3 %reduce-scatter.2.cloned.1.call-done = f32[512,1,256]{2,0,1:T(8,128)} async-done(((f32[512,2,256]{2,0,1:T(8,128)}), f32[512,1,256]{2,0,1:T(8,128)}) %reduce-scatter.2.cloned.1.call-update) | async-done | bytes 524304 | tf_op jit(solution)/shard_map/reduce_scatter | solution.py:80
  417.2 25.4 %all_gather.18 = f32[512,256]{1,0:T(8,128)S(1)} all-gather(f32[32,256]{1,0:T(8,128)S(1)} %slice.211), channel_id=1, replica_groups=mesh['half'=2,'row'=16,'col'=16] {'row'}, dimensions={0}, use_global_device_ids=true | all-gather | bytes 557056 | tf_op jit(solution)/shard_map/all_gather | solution.py:82
  443.3 44.9 %all-reduce.6.cloned.1.call-done = f32[512,32]{1,0:T(8,128)} async-done(((f32[512,32]{1,0:T(8,128)}), f32[512,32]{1,0:T(8,128)}) %all-reduce.6.cloned.1.call-update) | async-done | bytes 65552 | tf_op jit(solution)/shard_map/psum | solution.py:20
  490.3 5.7 all-to-all-start
  496.1 16.3 %all-to-all-done = f32[512,16,32]{0,2,1:T(8,128)S(1)} async-done(((f32[512,16,32]{0,2,1:T(8,128)}), f32[512,16,32]{0,2,1:T(8,128)S(1)}, u32[]{:S(2)}, u32[]{:S(2)}) %all-to-all-start) | async-done | bytes 1048608 | tf_op jit(solution)/shard_map/all_to_all | solution.py:13
  514.0 11.7 %cholesky.358 = f32[128,128]{1,0:T(8,128)S(1)} custom-call(f32[128,128]{1,0:T(8,128)S(1)} %cholesky.439), custom_call_target="Cholesky" | custom-call | tf_op jit(solution)/shard_map/jit(cholesky)/cholesky | solution.py:85
  525.9 9.8 %custom-call.36 = f32[1,128,128]{1,2,0:T(8,128)S(1)} custom-call(f32[1,128,128]{2,1,0:T(8,128)S(1)} %get-tuple-element.69), custom_call_target="InvertDiagBlocksLowerTriangular" | custom-call | tf_op jit(solution)/shard_map/jit(cholesky)/cholesky | solution.py:85
  538.2 11.7 %cholesky.377 = f32[128,128]{1,0:T(8,128)S(1)} custom-call(f32[128,128]{1,0:T(8,128)S(1)} %cholesky.443), custom_call_target="Cholesky" | custom-call | tf_op jit(solution)/shard_map/jit(cholesky)/cholesky | solution.py:85
  551.3 10.0 %custom-call.37 = f32[1,128,128]{1,2,0:T(8,128)S(1)} custom-call(f32[1,128,128]{2,1,0:T(8,128)S(1)} %get-tuple-element.66), custom_call_target="InvertDiagBlocksLowerTriangular" | custom-call | tf_op jit(solution)/shard_map/jit(cholesky)/cholesky | solution.py:85
  562.9 11.7 %cholesky.398 = f32[128,128]{1,0:T(8,128)S(1)} custom-call(f32[128,128]{1,0:T(8,128)S(1)} %cholesky.448), custom_call_target="Cholesky" | custom-call | tf_op jit(solution)/shard_map/jit(cholesky)/cholesky | solution.py:85
  575.3 9.8 %custom-call.38 = f32[1,128,128]{1,2,0:T(8,128)S(1)} custom-call(f32[1,128,128]{2,1,0:T(8,128)S(1)} %get-tuple-element.63), custom_call_target="InvertDiagBlocksLowerTriangular" | custom-call | tf_op jit(solution)/shard_map/jit(cholesky)/cholesky | solution.py:85
  586.5 11.7 %cholesky.415 = f32[128,128]{1,0:T(8,128)S(1)} custom-call(f32[128,128]{1,0:T(8,128)S(1)} %convolution_subtract_fusion.15), custom_call_target="Cholesky" | custom-call | tf_op jit(solution)/shard_map/jit(cholesky)/cholesky | solution.py:85
  601.9 8.0 while.5
  609.9 39.3 %custom-call.26 = f32[4,128,128]{1,2,0:T(8,128)S(1)} custom-call(f32[4,128,128]{2,1,0:T(8,128)S(1)} %get-tuple-element.20), custom_call_target="InvertDiagBlocksLowerTriangular" | custom-call | tf_op jit(solution)/shard_map/triangular_solve | solution.py:24
  653.3 113.8 %all-reduce.8.cloned.1.call-done = f32[512,1,256]{2,0,1:T(8,128)} async-done(((f32[512,1,256]{2,0,1:T(8,128)}), f32[512,1,256]{2,0,1:T(8,128)}) %all-reduce.8.cloned.1.call-update) | async-done | bytes 524304 | tf_op jit(solution)/shard_map/psum | solution.py:20
  767.2 2.0 fusion.23
  770.5 20.7 %all-gather.9.cloned.1.call-done = f32[512,2,256]{2,0,1:T(8,128)} async-done(((f32[512,1,256]{2,0,1:T(8,128)}), f32[512,2,256]{2,0,1:T(8,128)}) %all-gather.9.cloned.1.call-update) | async-done | bytes 1048592 | tf_op jit(solution)/shard_map/all_gather | solution.py:88
  (145 shorter events, 73.7 us)
Async XLA Ops:
  7.2 214.4 %all-gather.11.cloned.1.call-start = ((), (), s32[]{:S(2)}) async-start(), calls=%async_computation.7 | async-start | bytes 4210688 | tf_op jit(solution)/shard_map/all_gather | solution.py:57
  8.6 358.9 %all-gather.7.cloned.1.call-start = ((), (), s32[]{:S(2)}) async-start(), calls=%async_computation.2 | async-start | bytes 1114112 | tf_op jit(solution)/shard_map/all_gather | solution.py:67
  10.3 365.5 %all-gather.13.cloned.1.call-start = ((), (), s32[]{:S(2)}) async-start(), calls=%async_computation.8 | async-start | bytes 1114112 | tf_op jit(solution)/shard_map/all_gather | solution.py:56
  11.9 403.3 %reduce-scatter.2.cloned.1.call-start = ((), (), s32[]{:S(2)}) async-start(), calls=%async_computation.3 | async-start | bytes 1572864 | tf_op jit(solution)/shard_map/reduce_scatter | solution.py:80
  231.2 1.0 copy-start.1
  372.4 0.7 copy-start.4
  375.8 7.7 copy-start.5
  375.8 7.7 copy-start.9
  382.9 0.7 copy-start.6
  388.7 26.5 %copy-start.7 = (f32[512,1,1,256]{3,2,1,0:T(1,128)S(1)}, f32[512,1,1,256]{3,2,1,0:T(1,128)}, u32[]{:S(2)}) copy-start(f32[512,1,1,256]{3,2,1,0:T(1,128)} %param.8) | copy-start | bytes 1572868
  391.9 96.3 %all-reduce.6.cloned.1.call-start = ((), (), s32[]{:S(2)}) async-start(), calls=%async_computation.4 | async-start | bytes 524288 | tf_op jit(solution)/shard_map/psum | solution.py:20
  416.4 0.8 copy-start.2
  490.3 22.1 %all-to-all-start = ((f32[512,16,32]{0,2,1:T(8,128)}), f32[512,16,32]{0,2,1:T(8,128)S(1)}, u32[]{:S(2)}, u32[]{:S(2)}) async-start(f32[512,16,32]{0,2,1:T(8,128)} %tile.2), calls=%async_computation.1 | async-start | bytes 2097152 | tf_op jit(solution)/shard_map/all_to_all | solution.py:13
  496.1 271.1 %all-reduce.8.cloned.1.call-start = ((), (), s32[]{:S(2)}) async-start(), calls=%async_computation.5 | async-start | bytes 1048576 | tf_op jit(solution)/shard_map/psum | solution.py:20
  513.0 1.0 copy-start
  649.2 1.5 copy-start.8
  651.1 141.6 %copy-start.3 = (f32[512,256]{1,0:T(8,128)S(1)}, f32[512,256]{1,0:T(8,128)}, u32[]{:S(2)}) copy-start(f32[512,256]{1,0:T(8,128)} %copy-done.2) | copy-start | bytes 1572868
  653.3 137.9 %all-gather.9.cloned.1.call-start = ((), (), s32[]{:S(2)}) async-start(), calls=%async_computation.6 | async-start | bytes 1572864 | tf_op jit(solution)/shard_map/all_gather | solution.py:88
Sparse Core Ops, SparseCore 0:
  13.1 208.4 all-gather.10
  225.1 59.4 all-gather.6
  287.2 63.3 all-gather.12
  392.0 23.1 reduce-scatter.1
  443.4 44.7 all-reduce.5
  653.4 113.7 all-reduce.7
  769.4 21.7 all-gather.8
